TPU v7x, 32 devices: a whole 2x2x4 slice. The times are simulated.
32 devices in a mesh: groups: 2 (over x), shard: 8 (over z, y), replica: 2 (over core).
Axes of the slice: x: 2, y: 2, z: 4, core: 2. Of those that a mesh axis runs over, the one named last changes fastest.
Arguments:
- features: bfloat16 [16384, 5120], P(('groups', 'shard', 'replica')), parts along dimension 0, may hold values from -6 to 6
- cotangents: bfloat16 [16384, 2048], P(('groups', 'shard', 'replica')), parts along dimension 0, may hold values from -6 to 6
- feedback: float32 [2, 10240, 2048], P('replica', ('groups', 'shard')), parts along dimension 1, may hold values from -2 to 2
- factors: float32 [16, 2, 32, 1024], P(('groups', 'shard')), parts along dimension 0, may hold values from -0.1875 to 0.1875
Outputs:
- update: float32 [10240, 2048], P(('groups', 'shard')), parts along dimension 0
- new_feedback: float32 [2, 10240, 2048], P('replica', ('groups', 'shard')), parts along dimension 1
- next_factors: float32 [16, 2, 32, 1024], P(('groups', 'shard')), parts along dimension 0
There are 2 independent parts, one for each index of `groups`. A program takes and returns all parts, laid end to end along the dimension named above; each array names one. Nothing has to cross between parts.
All inputs are finite; a program needn't handle non-finite values.
Results may differ from a plain program's by a relative error of at most 0.012.
Values may be sent and summed in bfloat16 or wider, within the bound.
A program may use at most 128 MiB of HBM per device.

v0:
```python
import math

import jax
import jax.numpy as jnp
from jax import lax
from jax.sharding import PartitionSpec as P


def orthonormal(left):
    gram = jnp.einsum("...dq,...dp->...qp", left, left, precision=lax.Precision.HIGHEST)
    lower_part = jnp.linalg.cholesky(gram)
    return lax.linalg.triangular_solve(
        lower_part, left, left_side=False, lower=True, transpose_a=True
    )


def gradient_block(features, cot_part, grad_scale):

    def partial_term(start, count):
        product = lax.dot_general(
            features, cot_part, (((0,), (0,)), ((), ())), preferred_element_type=jnp.float32
        )
        return product * grad_scale

    return partial_term


def compress(matrix, old_right, replica_count):
    left = lax.dot_general(
        matrix,
        old_right,
        (((1,), (1,)), ((), ())),
        precision=lax.Precision.HIGHEST,
        preferred_element_type=jnp.float32,
    )
    left = lax.psum(left, "replica")
    basis = orthonormal(left)
    fresh = lax.dot_general(
        basis,
        matrix,
        (((0,), (0,)), ((), ())),
        precision=lax.Precision.HIGHEST,
        preferred_element_type=jnp.float32,
    )
    fresh = lax.psum(fresh, "replica")
    update = jnp.dot(basis, fresh, precision=lax.Precision.HIGHEST) / replica_count
    return (update, matrix - update, fresh)


def body(features, cotangents, feedback, factors):
    shard_count = lax.axis_size("shard")
    replica_count = lax.axis_size("replica")
    tok_count = features.shape[0]
    row_count = features.shape[1] // shard_count
    kv_width = factors.shape[3]
    grad_scale = 0.25 / math.sqrt(tok_count * shard_count)
    stored_error = feedback[0]
    results = []
    partial_term = gradient_block(features, cotangents, grad_scale)
    gradient = lax.psum_scatter(
        partial_term(jnp.int32(0), row_count * lax.axis_size("shard")).astype(jnp.bfloat16),
        "shard",
        scatter_dimension=0,
        tiled=True,
    ).astype(jnp.float32)
    merged_all = stored_error + gradient
    for member in range(2):
        merged = merged_all[:, member * kv_width : (member + 1) * kv_width]
        results.append(compress(merged, factors[0, member], replica_count))
    update = jnp.concatenate([results[0][0], results[1][0]], axis=1)
    new_feedback = jnp.concatenate([results[0][1], results[1][1]], axis=1)[None]
    next_factors = jnp.stack([results[0][2], results[1][2]], axis=0)[None]
    return (update, new_feedback, next_factors)


def solution(mesh):
    return jax.shard_map(
        body,
        mesh=mesh,
        in_specs=(
            P(("groups", "shard", "replica"), None),
            P(("groups", "shard", "replica"), None),
            P("replica", ("groups", "shard"), None),
            P(("groups", "shard"), None, None, None),
        ),
        out_specs=(
            P(("groups", "shard"), None),
            P("replica", ("groups", "shard"), None),
            P(("groups", "shard"), None, None, None),
        ),
        check_vma=False,
    )
```

profile of v0, /device:TPU:17, one launch (start us, length us, event | category | flops | bytes accessed | tf_op | source)
XLA Modules:
  0.0 466.9 jit_solution(12553580919800841582)
XLA Ops:
  7.2 0.0 reduce-scatter.2.cloned.1.call-start
  7.2 1.5 copy-done
  8.8 16.6 %multiply_convert_fusion = bf16[5120,2048]{1,0:T(8,128)(2,1)} fusion(bf16[512,5120]{1,0:T(8,128)(2,1)} %param.7, bf16[512,2048]{1,0:T(8,128)(2,1)S(1)} %copy-done), kind=kOutput, calls=%fused_computation | convolution fusion | flops 10758389760 | bytes 28311552 | tf_op jit(solution)/shard_map/dot_general | solution.py:20
  25.4 0.0 all-reduce.7.cloned.1.call-start
  25.4 344.4 %reduce-scatter.2.cloned.1.call-done = bf16[640,2048]{1,0:T(8,128)(2,1)} async-done(((bf16[5120,2048]{1,0:T(8,128)(2,1)}), bf16[640,2048]{1,0:T(8,128)(2,1)}) %reduce-scatter.2.cloned.1.call-update) | async-done | bytes 2621456 | tf_op jit(solution)/shard_map/reduce_scatter | solution.py:60
  369.8 4.1 bitcast_add_fusion
  374.0 3.1 fusion.2
  377.2 3.1 fusion.6
  380.3 0.2 all-reduce.5.cloned.1.call-start
  380.5 18.6 %all-reduce.7.cloned.1.call-done = (f32[640,32]{0,1:T(8,128)}, f32[640,32]{0,1:T(8,128)}) async-done(((f32[640,32]{0,1:T(8,128)}, f32[640,32]{0,1:T(8,128)}), (f32[640,32]{0,1:T(8,128)}, f32[640,32]{0,1:T(8,128)})) %all-reduce.7.cloned.1.call-update) | async-done | bytes 163856 | tf_op jit(solution)/shard_map/psum | solution.py:36
  399.2 1.2 fusion.19
  400.4 1.2 fusion.18
  401.5 0.1 copy.7
  401.6 2.9 cholesky.44
  404.6 0.6 compare_reduce_fusion.1
  405.2 0.7 fusion.12
  405.9 2.4 custom-call.6
  408.3 1.2 convolution_bitcast_fusion.1
  409.5 0.1 copy.8
  409.6 2.9 cholesky.55
  412.5 0.6 compare_reduce_fusion
  413.2 0.7 fusion.13
  413.8 2.4 custom-call.7
  416.3 1.2 convolution_bitcast_fusion
  417.5 4.0 fusion
  421.4 4.0 fusion.4
  425.5 19.6 %all-reduce.5.cloned.1.call-done = (f32[32,1024]{1,0:T(8,128)}, f32[32,1024]{1,0:T(8,128)}) async-done(((f32[32,1024]{1,0:T(8,128)}, f32[32,1024]{1,0:T(8,128)}), (f32[32,1024]{1,0:T(8,128)}, f32[32,1024]{1,0:T(8,128)})) %all-reduce.5.cloned.1.call-update) | async-done | bytes 262160 | tf_op jit(solution)/shard_map/psum | solution.py:45
  445.1 3.2 convolution_multiply_fusion
  448.3 5.4 %slice_subtract_fusion.1 = (f32[640,1024]{1,0:T(8,128)S(1)}, f32[640,1024]{1,0:T(8,128)S(1)}, f32[640,1024]{1,0:T(8,128)S(1)}) fusion(f32[640,2048]{1,0:T(8,128)} %copy-done.1, f32[640,1024]{1,0:T(8,128)S(1)} %convolution_multiply_fusion, f32[640,32]{0,1:T(8,128)S(1)} %convolution_bitcast_fusion.1, f32[32,1024]{1,0:T(8,128)S(1)} %copy-done.2), kind=kOutput, calls=%fused_computation.9 | convolution fusion | flops 253624320 | bytes 15941632 | tf_op jit(solution)/shard_map/dot_general | solution.py:46
  453.7 3.0 pad_maximum_fusion
  456.7 0.7 maximum_bitcast_fusion.1
  457.4 3.0 maximum_bitcast_fusion
  (16 shorter events, 0.2 us)
Async XLA Ops:
  7.2 1.6 copy-start
  7.2 362.7 %reduce-scatter.2.cloned.1.call-start = ((), (), s32[]{:S(2)}) async-start(), calls=%async_computation.1 | async-start | bytes 23592960 | tf_op jit(solution)/shard_map/reduce_scatter | solution.py:60
  25.3 348.7 %copy-start.4 = (f32[1,2,32,1024]{3,2,1,0:T(8,128)S(1)}, f32[1,2,32,1024]{3,2,1,0:T(8,128)}, u32[]{:S(2)}) copy-start(f32[1,2,32,1024]{3,2,1,0:T(8,128)} %param.10) | copy-start | bytes 786436
  25.4 373.8 %all-reduce.7.cloned.1.call-start = ((), (), s32[]{:S(2)}) async-start(), calls=%async_computation.3 | async-start | bytes 327680 | tf_op jit(solution)/shard_map/psum | solution.py:36
  374.0 3.1 copy-start.1
  380.3 64.8 %all-reduce.5.cloned.1.call-start = ((), (), s32[]{:S(2)}) async-start(), calls=%async_computation.2 | async-start | bytes 524288 | tf_op jit(solution)/shard_map/psum | solution.py:45
  445.1 3.2 copy-start.2
  453.7 3.0 copy-start.3
Sparse Core Ops, SparseCore 0:
  25.5 344.3 reduce-scatter.1
  380.4 18.6 all-reduce.6
  425.6 19.4 all-reduce.4
where the time goes:
time: 468 us; the launch traced here: 467 us
  waiting for transfers between devices  383 us (82%)
  matrix products  44.1 us (9%)
  other arithmetic  24.1 us (5%)
  between operations  13.9 us (3%)
    reduce_scatter x1, waiting for transfers between devices, body(): lax.psum_scatter(partial_term(jnp.int32(0), row_count * lax.axis_size('sh...  344 us
    psum x1, waiting for transfers between devices, compress(): fresh = lax.psum(fresh, 'replica')  19.6 us
    psum x1, waiting for transfers between devices, compress(): left = lax.psum(left, 'replica')  18.6 us
    dot_general x1, matrix products, partial_term(): lax.dot_general(features, cot_part, (((0,), (0,)), ((), ())), preferred_e...  16.6 us
  transfers between devices with their start and end apart: 3, of which 3 were waited for; matrix products, arithmetic and copies ran while one was open for 0% of the time, Pallas kernels for 0%

commit v1 on v0

--- a/solution.py
+++ b/solution.py
@@ -1,9 +1,15 @@
+import functools
 import math
 
 import jax
 import jax.numpy as jnp
 from jax import lax
+from jax.experimental import pallas as pl
+from jax.experimental.pallas import tpu as pltpu
 from jax.sharding import PartitionSpec as P
+
+COLS = 256
+MESH = pl.DeviceIdType.MESH
 
 
 def orthonormal(left):
@@ -14,15 +20,236 @@
     )
 
 
-def gradient_block(features, cot_part, grad_scale):
-
-    def partial_term(start, count):
-        product = lax.dot_general(
-            features, cot_part, (((0,), (0,)), ((), ())), preferred_element_type=jnp.float32
-        )
-        return product * grad_scale
-
-    return partial_term
+def merge_kernel(
+    lines, scale, by_slice, x_ref, g_ref, fb_ref, out_ref, xb, gb, up, down, acc,
+    sx_loc, sg_loc, sf_loc, sx_send, sx_recv, sg_send, sg_recv,
+    up_send, up_recv, down_send, down_recv, out_sem,
+):
+    tok = g_ref.shape[0]
+    rows = xb.shape[2]
+    chunks = gb.shape[0]
+    last = lines - 1
+    me = lax.axis_index("shard")
+    z = me // 2
+    y = me % 2
+    mate = {"shard": me + 1 - 2 * y}
+    above = {"shard": jnp.minimum(me + 2, 2 * lines - 2 + y)}
+    below = {"shard": jnp.maximum(me - 2, y)}
+    lower = z <= last - z
+    edge = jnp.minimum(z, last - z)
+
+    def x_part(block):
+        if by_slice:
+            return x_ref.at[:, pl.ds(pl.multiple_of(block * rows, rows), rows)]
+        return x_ref.at[block]
+
+    def g_part(c):
+        return g_ref.at[:, pl.ds(pl.multiple_of(c * COLS, COLS), COLS)]
+
+    def x_local(d):
+        return pltpu.make_async_copy(
+            x_part(2 * d + y), xb.at[d, pl.ds(0, tok)], sx_loc.at[d])
+
+    def x_remote(d):
+        return pltpu.make_async_remote_copy(
+            src_ref=x_part(2 * d + 1 - y), dst_ref=xb.at[d, pl.ds(tok, tok)],
+            send_sem=sx_send.at[d], recv_sem=sx_recv.at[d],
+            device_id=mate, device_id_type=MESH)
+
+    def g_local(c):
+        return pltpu.make_async_copy(g_part(c), gb.at[c, pl.ds(0, tok)], sg_loc.at[c])
+
+    def g_remote(c):
+        return pltpu.make_async_remote_copy(
+            src_ref=g_part(c), dst_ref=gb.at[c, pl.ds(tok, tok)],
+            send_sem=sg_send.at[c], recv_sem=sg_recv.at[c],
+            device_id=mate, device_id_type=MESH)
+
+    def hop(slots, send, recv, d, c, i, target):
+        return pltpu.make_async_remote_copy(
+            src_ref=slots.at[d, c], dst_ref=slots.at[d, c],
+            send_sem=send.at[i % 2], recv_sem=recv.at[d, c],
+            device_id=target, device_id_type=MESH)
+
+    def up_hop(i):
+        return hop(up, up_send, up_recv, last - i // chunks, i % chunks, i, above)
+
+    def down_hop(i):
+        return hop(down, down_send, down_recv, i // chunks, i % chunks, i, below)
+
+    fb_copy = pltpu.make_async_copy(fb_ref.at[0], acc, sf_loc)
+
+    barrier = pltpu.get_barrier_semaphore()
+    pl.semaphore_signal(barrier, inc=1, device_id=mate, device_id_type=MESH)
+
+    @pl.when(z < last)
+    def _():
+        pl.semaphore_signal(barrier, inc=1, device_id=above, device_id_type=MESH)
+
+    @pl.when(z > 0)
+    def _():
+        pl.semaphore_signal(barrier, inc=1, device_id=below, device_id_type=MESH)
+
+    pl.semaphore_wait(
+        barrier, 1 + jnp.where(z < last, 1, 0) + jnp.where(z > 0, 1, 0))
+
+    def start_x(d):
+        x_remote(d).start()
+        x_local(d).start()
+
+    def start_g(c):
+        g_remote(c).start()
+        g_local(c).start()
+
+    first = jnp.where(lower, last, 0)
+    second = jnp.where(lower, 0, last)
+    start_x(first)
+    start_g(0)
+
+    @pl.when(edge > 0)
+    def _():
+        start_x(second)
+
+    @pl.loop(1, chunks)
+    def _(c):
+        start_g(c)
+
+    @pl.loop(1, last)
+    def _(k):
+        @pl.when(last - k > z)
+        def _():
+            start_x(last - k)
+
+        @pl.when(k < z)
+        def _():
+            start_x(k)
+
+    start_x(z)
+    fb_copy.start()
+
+    def wait_x(d):
+        x_local(d).wait()
+        x_remote(d).wait()
+
+    def term(d, c):
+        return lax.dot_general(
+            xb[d], gb[c], (((0,), (0,)), ((), ())),
+            preferred_element_type=jnp.float32) * scale
+
+    def relay(slots, make, sends, i, d, c, inner):
+        @pl.when(c == 0)
+        def _():
+            wait_x(d)
+
+        value = term(d, c)
+
+        @pl.when(i >= 2)
+        def _():
+            make(i - 2).wait_send()
+
+        @pl.when(inner)
+        def _():
+            make(i).wait_recv()
+            slots[d, c] = (value + slots[d, c].astype(jnp.float32)).astype(slots.dtype)
+
+        @pl.when(jnp.logical_not(inner))
+        def _():
+            slots[d, c] = value.astype(slots.dtype)
+
+        make(i).start()
+
+    @pl.loop(edge, last * chunks + last)
+    def _(t):
+        @pl.when(t - edge < chunks)
+        def _():
+            g_local(t - edge).wait()
+            g_remote(t - edge).wait()
+
+        i = t - z
+
+        @pl.when(jnp.logical_and(i >= 0, i < (last - z) * chunks))
+        def _():
+            relay(up, up_hop, up_send, i, last - i // chunks, i % chunks, z > 0)
+
+        j = t - (last - z)
+
+        @pl.when(jnp.logical_and(j >= 0, j < z * chunks))
+        def _():
+            relay(down, down_hop, down_send, j, j // chunks, j % chunks, z < last)
+
+    wait_x(z)
+    fb_copy.wait()
+
+    def out_copy(c):
+        view = pl.ds(pl.multiple_of(c * COLS, COLS), COLS)
+        return pltpu.make_async_copy(
+            acc.at[:, view], out_ref.at[:, view], out_sem.at[c])
+
+    @pl.loop(0, chunks)
+    def _(c):
+        view = pl.ds(pl.multiple_of(c * COLS, COLS), COLS)
+        acc[:, view] += term(z, c)
+
+        @pl.when(z > 0)
+        def _():
+            up_hop((last - z) * chunks + c).wait_recv()
+            acc[:, view] += up[z, c].astype(jnp.float32)
+
+        @pl.when(z < last)
+        def _():
+            down_hop(z * chunks + c).wait_recv()
+            acc[:, view] += down[z, c].astype(jnp.float32)
+
+        out_copy(c).start()
+
+    @pl.loop(0, 2)
+    def _(k):
+        @pl.when(z < last)
+        def _():
+            up_hop((last - z) * chunks - 2 + k).wait_send()
+
+        @pl.when(z > 0)
+        def _():
+            down_hop(z * chunks - 2 + k).wait_send()
+
+    @pl.loop(0, chunks)
+    def _(c):
+        out_copy(c).wait()
+
+
+def merged_gradient(features, cotangents, feedback, scale):
+    shard_count = lax.axis_size("shard")
+    lines = shard_count // 2
+    tok, width = cotangents.shape
+    rows = features.shape[1] // shard_count
+    chunks = width // COLS
+    by_slice = rows % 128 == 0
+    if not by_slice:
+        features = features.reshape(tok, shard_count, rows).transpose(1, 0, 2)
+    dma = pltpu.SemaphoreType.DMA
+    bf16 = jnp.bfloat16
+    flops = 2 * tok * rows * shard_count * width
+    return pl.pallas_call(
+        functools.partial(merge_kernel, lines, scale, by_slice),
+        out_shape=jax.ShapeDtypeStruct((rows, width), jnp.float32),
+        in_specs=[pl.BlockSpec(memory_space=pl.ANY)] * 3,
+        out_specs=pl.BlockSpec(memory_space=pl.ANY),
+        scratch_shapes=[
+            pltpu.VMEM((lines, 2 * tok, rows), bf16),
+            pltpu.VMEM((chunks, 2 * tok, COLS), bf16),
+            pltpu.VMEM((lines, chunks, rows, COLS), bf16),
+            pltpu.VMEM((lines, chunks, rows, COLS), bf16),
+            pltpu.VMEM((rows, width), jnp.float32),
+            dma((lines,)), dma((chunks,)), dma,
+            dma((lines,)), dma((lines,)), dma((chunks,)), dma((chunks,)),
+            dma((2,)), dma((lines, chunks)), dma((2,)), dma((lines, chunks)),
+            dma((chunks,)),
+        ],
+        compiler_params=pltpu.CompilerParams(
+            collective_id=0, has_side_effects=True, vmem_limit_bytes=56 * 2**20),
+        cost_estimate=pl.CostEstimate(
+            flops=flops, bytes_accessed=20 * 2**20, transcendentals=0),
+    )(features, cotangents, feedback)
 
 
 def compress(matrix, old_right, replica_count):
@@ -50,20 +277,10 @@
 def body(features, cotangents, feedback, factors):
     shard_count = lax.axis_size("shard")
     replica_count = lax.axis_size("replica")
-    tok_count = features.shape[0]
-    row_count = features.shape[1] // shard_count
     kv_width = factors.shape[3]
-    grad_scale = 0.25 / math.sqrt(tok_count * shard_count)
-    stored_error = feedback[0]
+    grad_scale = 0.25 / math.sqrt(features.shape[0] * shard_count)
     results = []
-    partial_term = gradient_block(features, cotangents, grad_scale)
-    gradient = lax.psum_scatter(
-        partial_term(jnp.int32(0), row_count * lax.axis_size("shard")).astype(jnp.bfloat16),
-        "shard",
-        scatter_dimension=0,
-        tiled=True,
-    ).astype(jnp.float32)
-    merged_all = stored_error + gradient
+    merged_all = merged_gradient(features, cotangents, feedback, grad_scale)
     for member in range(2):
         merged = merged_all[:, member * kv_width : (member + 1) * kv_width]
         results.append(compress(merged, factors[0, member], replica_count))

time: 468 us -> 298 us (0.64)
  waiting for transfers between devices: 383 us -> 39.7 us
  Pallas kernels: 0 us -> 194 us
  matrix products: 44.1 us -> 29.2 us
    reduce_scatter x1 -> x0, waiting for transfers between devices: 344 us -> none  [body(): lax.psum_scatter(partial_term(jnp.int32(0), row_count * lax.axis_size('sh...]
    pallas_call x0 -> x1, Pallas kernels: none -> 194 us  [merged_gradient(): pl.pallas_call(functools.partial(merge_kernel, lines, scale, by_slice), o...]
    dot_general x1 -> x0, matrix products: 16.6 us -> none  [partial_term(): lax.dot_general(features, cot_part, (((0,), (0,)), ((), ())), preferred_e...]
  transfers between devices with their start and end apart: 3 -> 2, of which waited for: 3 -> 2; matrix products, arithmetic and copies ran while one was open for 0% -> 0% of each run, Pallas kernels for 0% -> 0%
where the time goes in v1:
time: 298 us; the launch traced here: 297 us
  Pallas kernels  194 us (65%)
  waiting for transfers between devices  39.7 us (13%)
  matrix products  29.2 us (10%)
  other arithmetic  20 us (7%)
  between operations  14.1 us (5%)
    pallas_call x1, Pallas kernels, merged_gradient(): pl.pallas_call(functools.partial(merge_kernel, lines, scale, by_slice), o...  194 us
    psum x1, waiting for transfers between devices, compress(): left = lax.psum(left, 'replica')  20 us
    psum x1, waiting for transfers between devices, compress(): fresh = lax.psum(fresh, 'replica')  19.6 us
    dot_general x2, matrix products, compress(): lax.dot_general(matrix, old_right, (((1,), (1,)), ((), ())), precision=la...  9.7 us
    dot_general x2, matrix products, compress(): jnp.dot(basis, fresh, precision=lax.Precision.HIGHEST) / replica_count  8.6 us
    dot_general x2, matrix products, compress(): lax.dot_general(basis, matrix, (((0,), (0,)), ((), ())), precision=lax.Pr...  7.98 us
    another operation x6, other arithmetic, orthonormal(): lower_part = jnp.linalg.cholesky(gram)  7.19 us
    another operation x4, other arithmetic, orthonormal(): lax.linalg.triangular_solve(lower_part, left, left_side=False, lower=True...  6.17 us
  transfers between devices with their start and end apart: 2, of which 2 were waited for; matrix products, arithmetic and copies ran while one was open for 0% of the time, Pallas kernels for 0%

profile of v1, /device:TPU:17, one launch (start us, length us, event | category | flops | bytes accessed | tf_op | source)
XLA Modules:
  0.0 297.0 jit_solution(18221669323756606618)
XLA Ops:
  7.2 0.0 copy-start.3
  7.2 0.0 all-reduce.7.cloned.1.call-start
  7.2 193.6 %shard_map.67 = f32[640,2048]{1,0:T(8,128)} custom-call(bf16[512,5120]{1,0:T(8,128)(2,1)} %x_ref.1, bf16[512,2048]{1,0:T(8,128)(2,1)} %g_ref.1, f32[1,640,2048]{2,1,0:T(8,128)} %fb_ref.1), custom_call_target="tpu_custom_call" | custom-call | flops 10737418240 | bytes 20971520 | tf_op jit(solution)/shard_map/pallas_call | solution.py:232
  200.8 0.0 copy-done.3
  200.8 4.9 %fusion.2 = f32[640,32]{0,1:T(8,128)} fusion(f32[640,2048]{1,0:T(8,128)} %shard_map.67, f32[1,2,32,1024]{3,2,1,0:T(8,128)S(1)} %copy-done.3), kind=kOutput, calls=%fused_computation.5 | convolution fusion | flops 251658240 | bytes 2834432 | tf_op jit(solution)/shard_map/dot_general | solution.py:256
  205.7 4.8 %fusion.6 = f32[640,32]{0,1:T(8,128)} fusion(f32[640,2048]{1,0:T(8,128)} %shard_map.67, f32[1,2,32,1024]{3,2,1,0:T(8,128)S(1)} %copy-done.3), kind=kOutput, calls=%fused_computation.10 | convolution fusion | flops 251658240 | bytes 2834432 | tf_op jit(solution)/shard_map/dot_general | solution.py:256
  210.6 0.0 all-reduce.7.cloned.1.call-update
  210.6 0.2 all-reduce.5.cloned.1.call-start
  210.8 20.0 %all-reduce.7.cloned.1.call-done = (f32[640,32]{0,1:T(8,128)}, f32[640,32]{0,1:T(8,128)}) async-done(((f32[640,32]{0,1:T(8,128)}, f32[640,32]{0,1:T(8,128)}), (f32[640,32]{0,1:T(8,128)}, f32[640,32]{0,1:T(8,128)})) %all-reduce.7.cloned.1.call-update) | async-done | bytes 163856 | tf_op jit(solution)/shard_map/psum | solution.py:263
  230.8 1.2 fusion.18
  232.0 0.1 copy.7
  232.1 2.9 cholesky.44
  235.1 0.6 compare_reduce_fusion.1
  235.7 0.7 fusion.12
  236.4 2.4 custom-call.6
  238.8 1.2 convolution_bitcast_fusion.1
  240.0 4.0 %fusion.4 = f32[32,1024]{1,0:T(8,128)} fusion(f32[640,32]{0,1:T(8,128)S(1)} %convolution_bitcast_fusion.1, f32[640,2048]{1,0:T(8,128)} %shard_map.67), kind=kOutput, calls=%fused_computation.8 | convolution fusion | flops 251658240 | bytes 2834432 | tf_op jit(solution)/shard_map/dot_general | solution.py:265
  244.0 0.2 fusion.19
  244.2 0.1 copy.8
  244.3 2.9 cholesky.55
  247.2 0.6 compare_reduce_fusion
  247.9 0.7 fusion.13
  248.5 2.4 custom-call.7
  251.0 0.3 convolution_bitcast_fusion
  251.3 4.0 %fusion = f32[32,1024]{1,0:T(8,128)} fusion(f32[640,32]{0,1:T(8,128)S(1)} %convolution_bitcast_fusion, f32[640,2048]{1,0:T(8,128)} %shard_map.67), kind=kOutput, calls=%fused_computation.3 | convolution fusion | flops 251658240 | bytes 2834432 | tf_op jit(solution)/shard_map/dot_general | solution.py:265
  255.3 0.0 all-reduce.5.cloned.1.call-update
  255.3 19.6 %all-reduce.5.cloned.1.call-done = (f32[32,1024]{1,0:T(8,128)}, f32[32,1024]{1,0:T(8,128)}) async-done(((f32[32,1024]{1,0:T(8,128)}, f32[32,1024]{1,0:T(8,128)}), (f32[32,1024]{1,0:T(8,128)}, f32[32,1024]{1,0:T(8,128)})) %all-reduce.5.cloned.1.call-update) | async-done | bytes 262160 | tf_op jit(solution)/shard_map/psum | solution.py:272
  274.9 3.2 %convolution_multiply_fusion = f32[640,1024]{1,0:T(8,128)S(1)} fusion(f32[640,32]{0,1:T(8,128)S(1)} %convolution_bitcast_fusion, f32[32,1024]{1,0:T(8,128)} %get-tuple-element.5), kind=kOutput, calls=%fused_computation.12 | convolution fusion | flops 252313600 | bytes 2834432 | tf_op jit(solution)/shard_map/dot_general | solution.py:273
  278.1 5.4 %slice_subtract_fusion.1 = (f32[640,1024]{1,0:T(8,128)S(1)}, f32[640,1024]{1,0:T(8,128)S(1)}, f32[640,1024]{1,0:T(8,128)S(1)}) fusion(f32[640,2048]{1,0:T(8,128)} %shard_map.67, f32[640,1024]{1,0:T(8,128)S(1)} %convolution_multiply_fusion, f32[640,32]{0,1:T(8,128)S(1)} %convolution_bitcast_fusion.1, f32[32,1024]{1,0:T(8,128)S(1)} %copy-done.1), kind=kOutput, calls=%fused_computation.7 | convolution fusion | flops 253624320 | bytes 15941632 | tf_op jit(solution)/shard_map/dot_general | solution.py:273
  283.5 3.0 pad_maximum_fusion
  286.5 3.0 maximum_bitcast_fusion
  289.5 0.7 maximum_bitcast_fusion.1
  (10 shorter events, 0.1 us)
Async XLA Ops:
  7.2 193.7 %copy-start.3 = (f32[1,2,32,1024]{3,2,1,0:T(8,128)S(1)}, f32[1,2,32,1024]{3,2,1,0:T(8,128)}, u32[]{:S(2)}) copy-start(f32[1,2,32,1024]{3,2,1,0:T(8,128)} %param.10) | copy-start | bytes 786436
  7.2 223.7 %all-reduce.7.cloned.1.call-start = ((), (), s32[]{:S(2)}) async-start(), calls=%async_computation.1 | async-start | bytes 327680 | tf_op jit(solution)/shard_map/psum | solution.py:263
  210.6 64.3 %all-reduce.5.cloned.1.call-start = ((), (), s32[]{:S(2)}) async-start(), calls=%async_computation | async-start | bytes 524288 | tf_op jit(solution)/shard_map/psum | solution.py:272
  230.8 13.1 %copy-start = (f32[640,32]{0,1:T(8,128)S(1)}, f32[640,32]{0,1:T(8,128)}, u32[]{:S(2)}) copy-start(f32[640,32]{0,1:T(8,128)} %get-tuple-element.7) | copy-start | bytes 245764
  274.9 3.2 %copy-start.1 = (f32[32,1024]{1,0:T(8,128)S(1)}, f32[32,1024]{1,0:T(8,128)}, u32[]{:S(2)}) copy-start(f32[32,1024]{1,0:T(8,128)} %get-tuple-element.6) | copy-start | bytes 393220
  286.5 3.0 copy-start.2
Sparse Core Ops, SparseCore 0:
  210.7 20.0 all-reduce.6
  255.4 19.4 all-reduce.4

commit v2 on v1

--- a/solution.py
+++ b/solution.py
@@ -12,21 +12,44 @@
 MESH = pl.DeviceIdType.MESH
 
 
-def orthonormal(left):
-    gram = jnp.einsum("...dq,...dp->...qp", left, left, precision=lax.Precision.HIGHEST)
-    lower_part = jnp.linalg.cholesky(gram)
-    return lax.linalg.triangular_solve(
-        lower_part, left, left_side=False, lower=True, transpose_a=True
-    )
+def halves(value):
+    high = value.astype(jnp.bfloat16)
+    return high, (value - high.astype(jnp.float32)).astype(jnp.bfloat16)
+
+
+def dot_t(a, b):
+    return lax.dot_general(
+        a, b, (((1,), (1,)), ((), ())), preferred_element_type=jnp.float32)
+
+
+def inverse_factor(gram):
+    rank = gram.shape[0]
+    row_at = lax.broadcasted_iota(jnp.int32, (rank, rank), 0)
+    col_at = lax.broadcasted_iota(jnp.int32, (rank, rank), 1)
+    eye = jnp.where(row_at == col_at, 1.0, 0.0)
+    table = jnp.concatenate([gram, eye], axis=1)
+    index = lax.broadcasted_iota(jnp.int32, (rank, 1), 0)
+    for j in range(rank):
+        row = table[j : j + 1, :]
+        ratio = table[:, j : j + 1] / table[j : j + 1, j : j + 1]
+        table = table - jnp.where(index > j, ratio, 0.0) * row
+    pivots = jnp.sum(table[:, :rank] * eye, axis=1, keepdims=True)
+    return table[:, rank:] / jnp.sqrt(pivots)
 
 
 def merge_kernel(
-    lines, scale, by_slice, x_ref, g_ref, fb_ref, out_ref, xb, gb, up, down, acc,
+    lines, scale, by_slice, x_ref, g_ref, fb_ref, f_ref,
+    out_ref, fresh_ref, b3_ref, f3_ref,
+    xb, gb, up, down, acc, high, low, left, left_in, fresh, fresh_in,
+    left_send, left_recv, fresh_send, fresh_recv,
     sx_loc, sg_loc, sf_loc, sx_send, sx_recv, sg_send, sg_recv,
     up_send, up_recv, down_send, down_recv, out_sem,
 ):
     tok = g_ref.shape[0]
     rows = xb.shape[2]
+    members, rank = f_ref.shape[1], f_ref.shape[2]
+    per = f_ref.shape[3] // COLS
+    twin = {"replica": 1 - lax.axis_index("replica")}
     chunks = gb.shape[0]
     last = lines - 1
     me = lax.axis_index("shard")
@@ -81,6 +104,7 @@
 
     barrier = pltpu.get_barrier_semaphore()
     pl.semaphore_signal(barrier, inc=1, device_id=mate, device_id_type=MESH)
+    pl.semaphore_signal(barrier, inc=1, device_id=twin, device_id_type=MESH)
 
     @pl.when(z < last)
     def _():
@@ -91,7 +115,7 @@
         pl.semaphore_signal(barrier, inc=1, device_id=below, device_id_type=MESH)
 
     pl.semaphore_wait(
-        barrier, 1 + jnp.where(z < last, 1, 0) + jnp.where(z > 0, 1, 0))
+        barrier, 2 + jnp.where(z < last, 1, 0) + jnp.where(z > 0, 1, 0))
 
     def start_x(d):
         x_remote(d).start()
@@ -179,6 +203,7 @@
 
     wait_x(z)
     fb_copy.wait()
+    left[...] = jnp.zeros_like(left)
 
     def out_copy(c):
         view = pl.ds(pl.multiple_of(c * COLS, COLS), COLS)
@@ -201,6 +226,60 @@
             acc[:, view] += down[z, c].astype(jnp.float32)
 
         out_copy(c).start()
+        hi, lo = halves(acc[:, view])
+        high[c] = hi
+        low[c] = lo
+        member = c // per
+        part = f_ref[0, member, :, pl.ds(pl.multiple_of(c % per * COLS, COLS), COLS)]
+        wide = jnp.concatenate(
+            [jnp.where(member == m, part, 0.0) for m in range(members)], axis=0)
+        f_hi, f_lo = halves(wide)
+        left[...] += dot_t(hi, f_hi) + dot_t(hi, f_lo) + dot_t(lo, f_hi)
+
+    left_copy = pltpu.make_async_remote_copy(
+        src_ref=left, dst_ref=left_in, send_sem=left_send, recv_sem=left_recv,
+        device_id=twin, device_id_type=MESH)
+    left_copy.start()
+    left_copy.wait()
+    total = left[...] + left_in[...]
+    gram = lax.dot_general(
+        total, total, (((0,), (0,)), ((), ())),
+        precision=lax.Precision.HIGHEST, preferred_element_type=jnp.float32)
+    empty = jnp.zeros((rank, rank), jnp.float32)
+    inverse = jnp.concatenate([
+        jnp.concatenate([
+            inverse_factor(gram[m * rank : (m + 1) * rank, m * rank : (m + 1) * rank])
+            if m == n else empty for n in range(members)], axis=1)
+        for m in range(members)], axis=0)
+    basis = lax.dot_general(
+        total, inverse, (((1,), (1,)), ((), ())),
+        precision=lax.Precision.HIGHEST, preferred_element_type=jnp.float32)
+    b_hi, b_lo = halves(jnp.swapaxes(basis, 0, 1))
+    for m in range(members):
+        span = slice(m * rank, (m + 1) * rank)
+        b3_ref[m] = jnp.concatenate([b_hi[span], b_hi[span], b_lo[span]], axis=0)
+
+    def fresh_copy(c):
+        return pltpu.make_async_remote_copy(
+            src_ref=fresh.at[c], dst_ref=fresh_in.at[c],
+            send_sem=fresh_send.at[c], recv_sem=fresh_recv.at[c],
+            device_id=twin, device_id_type=MESH)
+
+    @pl.loop(0, chunks)
+    def _(c):
+        both = b3_ref[c // per]
+        top = jnp.dot(both[rank:], high[c], preferred_element_type=jnp.float32)
+        rest = jnp.dot(both[:rank], low[c], preferred_element_type=jnp.float32)
+        fresh[c] = top[:rank] + top[rank:] + rest
+        fresh_copy(c).start()
+
+    for c in range(chunks):
+        fresh_copy(c).wait()
+        view = slice(c % per * COLS, (c % per + 1) * COLS)
+        whole = fresh[c] + fresh_in[c]
+        fresh_ref[0, c // per, :, view] = whole
+        w_hi, w_lo = halves(whole)
+        f3_ref[c // per, :, view] = jnp.concatenate([w_hi, w_lo, w_hi], axis=0)
 
     @pl.loop(0, 2)
     def _(k):
@@ -217,76 +296,91 @@
         out_copy(c).wait()
 
 
-def merged_gradient(features, cotangents, feedback, scale):
+def compress(features, cotangents, feedback, factors, scale):
     shard_count = lax.axis_size("shard")
     lines = shard_count // 2
     tok, width = cotangents.shape
     rows = features.shape[1] // shard_count
+    members, rank, kv_width = factors.shape[1:]
     chunks = width // COLS
     by_slice = rows % 128 == 0
     if not by_slice:
         features = features.reshape(tok, shard_count, rows).transpose(1, 0, 2)
     dma = pltpu.SemaphoreType.DMA
-    bf16 = jnp.bfloat16
+    bf16, f32 = jnp.bfloat16, jnp.float32
     flops = 2 * tok * rows * shard_count * width
+    vmem = pl.BlockSpec(memory_space=pltpu.VMEM)
+    anywhere = pl.BlockSpec(memory_space=pl.ANY)
     return pl.pallas_call(
         functools.partial(merge_kernel, lines, scale, by_slice),
-        out_shape=jax.ShapeDtypeStruct((rows, width), jnp.float32),
-        in_specs=[pl.BlockSpec(memory_space=pl.ANY)] * 3,
-        out_specs=pl.BlockSpec(memory_space=pl.ANY),
+        out_shape=[
+            jax.ShapeDtypeStruct((rows, width), f32),
+            jax.ShapeDtypeStruct(factors.shape, f32),
+            jax.ShapeDtypeStruct((members, 3 * rank, rows), bf16),
+            jax.ShapeDtypeStruct((members, 3 * rank, kv_width), bf16),
+        ],
+        in_specs=[anywhere] * 3 + [vmem],
+        out_specs=[anywhere, vmem, vmem, vmem],
         scratch_shapes=[
             pltpu.VMEM((lines, 2 * tok, rows), bf16),
             pltpu.VMEM((chunks, 2 * tok, COLS), bf16),
             pltpu.VMEM((lines, chunks, rows, COLS), bf16),
             pltpu.VMEM((lines, chunks, rows, COLS), bf16),
-            pltpu.VMEM((rows, width), jnp.float32),
+            pltpu.VMEM((rows, width), f32),
+            pltpu.VMEM((chunks, rows, COLS), bf16),
+            pltpu.VMEM((chunks, rows, COLS), bf16),
+            pltpu.VMEM((rows, members * rank), f32),
+            pltpu.VMEM((rows, members * rank), f32),
+            pltpu.VMEM((chunks, rank, COLS), f32),
+            pltpu.VMEM((chunks, rank, COLS), f32),
+            dma, dma, dma((chunks,)), dma((chunks,)),
             dma((lines,)), dma((chunks,)), dma,
             dma((lines,)), dma((lines,)), dma((chunks,)), dma((chunks,)),
             dma((2,)), dma((lines, chunks)), dma((2,)), dma((lines, chunks)),
             dma((chunks,)),
         ],
         compiler_params=pltpu.CompilerParams(
-            collective_id=0, has_side_effects=True, vmem_limit_bytes=56 * 2**20),
+            collective_id=0, has_side_effects=True, vmem_limit_bytes=58 * 2**20),
         cost_estimate=pl.CostEstimate(
             flops=flops, bytes_accessed=20 * 2**20, transcendentals=0),
-    )(features, cotangents, feedback)
-
-
-def compress(matrix, old_right, replica_count):
-    left = lax.dot_general(
-        matrix,
-        old_right,
-        (((1,), (1,)), ((), ())),
-        precision=lax.Precision.HIGHEST,
-        preferred_element_type=jnp.float32,
-    )
-    left = lax.psum(left, "replica")
-    basis = orthonormal(left)
-    fresh = lax.dot_general(
-        basis,
-        matrix,
-        (((0,), (0,)), ((), ())),
-        precision=lax.Precision.HIGHEST,
-        preferred_element_type=jnp.float32,
-    )
-    fresh = lax.psum(fresh, "replica")
-    update = jnp.dot(basis, fresh, precision=lax.Precision.HIGHEST) / replica_count
-    return (update, matrix - update, fresh)
+    )(features, cotangents, feedback, factors)
+
+
+def spread_kernel(replica_count, b3_ref, f3_ref, merged_ref, update_ref, rest_ref):
+    product = lax.dot_general(
+        b3_ref[0], f3_ref[0], (((0,), (0,)), ((), ())),
+        preferred_element_type=jnp.float32)
+    update = product / replica_count
+    update_ref[...] = update
+    rest_ref[0] = merged_ref[...] - update
+
+
+def spread(b3, f3, merged, replica_count):
+    rows, width = merged.shape
+    per = f3.shape[2] // COLS
+    cols = pl.BlockSpec((rows, COLS), lambda c: (0, c))
+    return pl.pallas_call(
+        functools.partial(spread_kernel, replica_count),
+        grid=(width // COLS,),
+        out_shape=[
+            jax.ShapeDtypeStruct((rows, width), jnp.float32),
+            jax.ShapeDtypeStruct((1, rows, width), jnp.float32),
+        ],
+        in_specs=[
+            pl.BlockSpec((1,) + b3.shape[1:], lambda c: (c // per, 0, 0)),
+            pl.BlockSpec((1, f3.shape[1], COLS), lambda c: (c // per, 0, c % per)),
+            cols,
+        ],
+        out_specs=[cols, pl.BlockSpec((1, rows, COLS), lambda c: (0, 0, c))],
+        compiler_params=pltpu.CompilerParams(vmem_limit_bytes=32 * 2**20),
+    )(b3, f3, merged)
 
 
 def body(features, cotangents, feedback, factors):
-    shard_count = lax.axis_size("shard")
-    replica_count = lax.axis_size("replica")
-    kv_width = factors.shape[3]
-    grad_scale = 0.25 / math.sqrt(features.shape[0] * shard_count)
-    results = []
-    merged_all = merged_gradient(features, cotangents, feedback, grad_scale)
-    for member in range(2):
-        merged = merged_all[:, member * kv_width : (member + 1) * kv_width]
-        results.append(compress(merged, factors[0, member], replica_count))
-    update = jnp.concatenate([results[0][0], results[1][0]], axis=1)
-    new_feedback = jnp.concatenate([results[0][1], results[1][1]], axis=1)[None]
-    next_factors = jnp.stack([results[0][2], results[1][2]], axis=0)[None]
+    grad_scale = 0.25 / math.sqrt(features.shape[0] * lax.axis_size("shard"))
+    merged, next_factors, b3, f3 = compress(
+        features, cotangents, feedback, factors, grad_scale)
+    update, new_feedback = spread(b3, f3, merged, lax.axis_size("replica"))
     return (update, new_feedback, next_factors)
 
 

time: 298 us -> 218 us (0.73)
  waiting for transfers between devices: 39.7 us -> 0 us
  matrix products: 29.2 us -> 0 us
  other arithmetic: 20 us -> 0 us
  Pallas kernels: 194 us -> 212 us
  between operations: 14.1 us -> 0.65 us
  local copies, waits for them, and re-layouts: 0.16 us -> 5.12 us
    psum x2 -> x0, waiting for transfers between devices: 39.7 us -> none  [the longest x1 20 us: compress(): left = lax.psum(left, 'replica')]
    dot_general x8 -> x0, matrix products: 27.7 us -> none  [the longest x2 9.7 us: compress(): lax.dot_general(matrix, old_right, (((1,), (1,)), ((), ())), precision=la...]
    pallas_call x1 -> x2, Pallas kernels: 194 us -> 212 us  [the longest x1 206 us: compress(): pl.pallas_call(functools.partial(merge_kernel, lines, scale, by_slice), o...]
    another operation x10 -> x0, other arithmetic: 13.4 us -> none  [the longest x6 7.19 us: orthonormal(): lower_part = jnp.linalg.cholesky(gram)]
    unnamed x8 -> x9, local copies, waits for them, and re-layouts: 0.02 us -> 5.12 us
    broadcast_in_dim x2 -> x0, other arithmetic: 3.67 us -> none  [the longest x1 2.95 us: body(): new_feedback = jnp.concatenate([results[0][1], results[1][1]], axis=1)[None]]
  transfers between devices with their start and end apart: 2 -> 0, of which waited for: 2 -> 0; matrix products, arithmetic and copies ran while one was open for 0% -> 0% of each run, Pallas kernels for 0% -> 0%
where the time goes in v2:
time: 218 us
  Pallas kernels  212 us (97%)
  local copies, waits for them, and re-layouts  5.12 us (2%)
    pallas_call x1, Pallas kernels, compress(): pl.pallas_call(functools.partial(merge_kernel, lines, scale, by_slice), o...  206 us
    pallas_call x1, Pallas kernels, spread(): pl.pallas_call(functools.partial(spread_kernel, replica_count), grid=(wid...  6.03 us
    unnamed x9, local copies, waits for them, and re-layouts  5.12 us

profile of v2, /device:TPU:17, one launch (start us, length us, event | category | flops | bytes accessed | tf_op | source)
XLA Modules:
  0.0 217.6 jit_solution(17980479227992730694)
XLA Ops:
  0.6 205.8 %shard_map.67 = (f32[640,2048]{1,0:T(8,128)}, f32[1,2,32,1024]{3,2,1,0:T(8,128)}, bf16[2,96,640]{2,1,0:T(8,128)(2,1)}, bf16[2,96,1024]{2,1,0:T(8,128)(2,1)}) custom-call(bf16[512,5120]{1,0:T(8,128)(2,1)} %x_ref.1, bf16[512,2048]{1,0:T(8,128)(2,1)} %g_ref.1, f32[1,640,2048]{2,1,0:T(8,128)} %fb_ref.1, f32[1,2,32,1024]{3,2,1,0:T(8,128)} %f_ref.1), custom_call_target="tpu_custom_call" | custom-call | flops 10737418240 | bytes 20971520 | tf_op jit(solution)/shard_map/pallas_call | solution.py:314
  206.5 0.0 copy-start
  206.5 2.5 %copy-done = f32[640,2048]{1,0:T(8,128)S(1)} copy-done((f32[640,2048]{1,0:T(8,128)S(1)}, f32[640,2048]{1,0:T(8,128)}, u32[]{:S(2)}) %copy-start) | copy-done | bytes 5242904
  208.9 0.0 copy-start.1
  208.9 1.0 copy-done.1
  209.9 0.0 copy-start.2
  209.9 0.9 copy-done.2
  210.9 0.0 copy-start.3
  210.9 6.0 %shard_map.68 = (f32[640,2048]{1,0:T(8,128)}, f32[1,640,2048]{2,1,0:T(8,128)}) custom-call(bf16[2,96,640]{2,1,0:T(8,128)(2,1)S(1)} %copy-done.2, bf16[2,96,1024]{2,1,0:T(8,128)(2,1)S(1)} %copy-done.1, f32[640,2048]{1,0:T(8,128)S(1)} %copy-done), custom_call_target="tpu_custom_call" | custom-call | tf_op jit(solution)/shard_map/pallas_call | solution.py:362
  216.9 0.0 copy-done.3
  216.9 0.7 copy.8
Async XLA Ops:
  206.5 2.5 %copy-start = (f32[640,2048]{1,0:T(8,128)S(1)}, f32[640,2048]{1,0:T(8,128)}, u32[]{:S(2)}) copy-start(f32[640,2048]{1,0:T(8,128)} %get-tuple-element.11.merged_ref) | copy-start | bytes 15728644
  208.9 1.0 copy-start.1
  209.9 0.9 copy-start.2
  210.9 6.0 %copy-start.3 = (f32[1,2,32,1024]{3,2,1,0:T(8,128)S(1)}, f32[1,2,32,1024]{3,2,1,0:T(8,128)}, u32[]{:S(2)}) copy-start(f32[1,2,32,1024]{3,2,1,0:T(8,128)} %get-tuple-element.20) | copy-start | bytes 786436

commit v3 on v2

--- a/solution.py
+++ b/solution.py
@@ -8,7 +8,9 @@
 from jax.experimental.pallas import tpu as pltpu
 from jax.sharding import PartitionSpec as P
 
-COLS = 256
+COLS = 128
+WIDE = 256
+DEPTH = 4
 MESH = pl.DeviceIdType.MESH
 
 
@@ -39,8 +41,8 @@
 
 def merge_kernel(
     lines, scale, by_slice, x_ref, g_ref, fb_ref, f_ref,
-    out_ref, fresh_ref, b3_ref, f3_ref,
-    xb, gb, up, down, acc, high, low, left, left_in, fresh, fresh_in,
+    out_ref, fresh_ref, b3_ref,
+    xb, xt, gb, up, down, acc, high, low, left, left_in, fresh, fresh_in,
     left_send, left_recv, fresh_send, fresh_recv,
     sx_loc, sg_loc, sf_loc, sx_send, sx_recv, sg_send, sg_recv,
     up_send, up_recv, down_send, down_recv, out_sem,
@@ -91,7 +93,7 @@
     def hop(slots, send, recv, d, c, i, target):
         return pltpu.make_async_remote_copy(
             src_ref=slots.at[d, c], dst_ref=slots.at[d, c],
-            send_sem=send.at[i % 2], recv_sem=recv.at[d, c],
+            send_sem=send.at[i % DEPTH], recv_sem=recv.at[d, c],
             device_id=target, device_id_type=MESH)
 
     def up_hop(i):
@@ -154,11 +156,10 @@
     def wait_x(d):
         x_local(d).wait()
         x_remote(d).wait()
+        xt[d] = jnp.swapaxes(xb[d], 0, 1)
 
     def term(d, c):
-        return lax.dot_general(
-            xb[d], gb[c], (((0,), (0,)), ((), ())),
-            preferred_element_type=jnp.float32) * scale
+        return jnp.dot(xt[d], gb[c], preferred_element_type=jnp.float32) * scale
 
     def relay(slots, make, sends, i, d, c, inner):
         @pl.when(c == 0)
@@ -167,9 +168,9 @@
 
         value = term(d, c)
 
-        @pl.when(i >= 2)
-        def _():
-            make(i - 2).wait_send()
+        @pl.when(i >= DEPTH)
+        def _():
+            make(i - DEPTH).wait_send()
 
         @pl.when(inner)
         def _():
@@ -227,8 +228,9 @@
 
         out_copy(c).start()
         hi, lo = halves(acc[:, view])
-        high[c] = hi
-        low[c] = lo
+        lanes = pl.ds(pl.multiple_of(c * COLS % WIDE, COLS), COLS)
+        high[c * COLS // WIDE, :, lanes] = hi
+        low[c * COLS // WIDE, :, lanes] = lo
         member = c // per
         part = f_ref[0, member, :, pl.ds(pl.multiple_of(c % per * COLS, COLS), COLS)]
         wide = jnp.concatenate(
@@ -265,31 +267,31 @@
             send_sem=fresh_send.at[c], recv_sem=fresh_recv.at[c],
             device_id=twin, device_id_type=MESH)
 
-    @pl.loop(0, chunks)
+    wide_count = high.shape[0]
+    wide_per = wide_count // members
+
+    @pl.loop(0, wide_count)
     def _(c):
-        both = b3_ref[c // per]
+        both = b3_ref[c // wide_per]
         top = jnp.dot(both[rank:], high[c], preferred_element_type=jnp.float32)
         rest = jnp.dot(both[:rank], low[c], preferred_element_type=jnp.float32)
         fresh[c] = top[:rank] + top[rank:] + rest
         fresh_copy(c).start()
 
-    for c in range(chunks):
+    for c in range(wide_count):
         fresh_copy(c).wait()
-        view = slice(c % per * COLS, (c % per + 1) * COLS)
-        whole = fresh[c] + fresh_in[c]
-        fresh_ref[0, c // per, :, view] = whole
-        w_hi, w_lo = halves(whole)
-        f3_ref[c // per, :, view] = jnp.concatenate([w_hi, w_lo, w_hi], axis=0)
-
-    @pl.loop(0, 2)
+        view = slice(c % wide_per * WIDE, (c % wide_per + 1) * WIDE)
+        fresh_ref[0, c // wide_per, :, view] = fresh[c] + fresh_in[c]
+
+    @pl.loop(0, DEPTH)
     def _(k):
         @pl.when(z < last)
         def _():
-            up_hop((last - z) * chunks - 2 + k).wait_send()
+            up_hop((last - z) * chunks - DEPTH + k).wait_send()
 
         @pl.when(z > 0)
         def _():
-            down_hop(z * chunks - 2 + k).wait_send()
+            down_hop(z * chunks - DEPTH + k).wait_send()
 
     @pl.loop(0, chunks)
     def _(c):
@@ -301,7 +303,7 @@
     lines = shard_count // 2
     tok, width = cotangents.shape
     rows = features.shape[1] // shard_count
-    members, rank, kv_width = factors.shape[1:]
+    members, rank = factors.shape[1:3]
     chunks = width // COLS
     by_slice = rows % 128 == 0
     if not by_slice:
@@ -317,26 +319,26 @@
             jax.ShapeDtypeStruct((rows, width), f32),
             jax.ShapeDtypeStruct(factors.shape, f32),
             jax.ShapeDtypeStruct((members, 3 * rank, rows), bf16),
-            jax.ShapeDtypeStruct((members, 3 * rank, kv_width), bf16),
         ],
         in_specs=[anywhere] * 3 + [vmem],
-        out_specs=[anywhere, vmem, vmem, vmem],
+        out_specs=[anywhere, vmem, vmem],
         scratch_shapes=[
             pltpu.VMEM((lines, 2 * tok, rows), bf16),
+            pltpu.VMEM((lines, rows, 2 * tok), bf16),
             pltpu.VMEM((chunks, 2 * tok, COLS), bf16),
             pltpu.VMEM((lines, chunks, rows, COLS), bf16),
             pltpu.VMEM((lines, chunks, rows, COLS), bf16),
             pltpu.VMEM((rows, width), f32),
-            pltpu.VMEM((chunks, rows, COLS), bf16),
-            pltpu.VMEM((chunks, rows, COLS), bf16),
+            pltpu.VMEM((width // WIDE, rows, WIDE), bf16),
+            pltpu.VMEM((width // WIDE, rows, WIDE), bf16),
             pltpu.VMEM((rows, members * rank), f32),
             pltpu.VMEM((rows, members * rank), f32),
-            pltpu.VMEM((chunks, rank, COLS), f32),
-            pltpu.VMEM((chunks, rank, COLS), f32),
-            dma, dma, dma((chunks,)), dma((chunks,)),
+            pltpu.VMEM((width // WIDE, rank, WIDE), f32),
+            pltpu.VMEM((width // WIDE, rank, WIDE), f32),
+            dma, dma, dma((width // WIDE,)), dma((width // WIDE,)),
             dma((lines,)), dma((chunks,)), dma,
             dma((lines,)), dma((lines,)), dma((chunks,)), dma((chunks,)),
-            dma((2,)), dma((lines, chunks)), dma((2,)), dma((lines, chunks)),
+            dma((DEPTH,)), dma((lines, chunks)), dma((DEPTH,)), dma((lines, chunks)),
             dma((chunks,)),
         ],
         compiler_params=pltpu.CompilerParams(
@@ -346,41 +348,49 @@
     )(features, cotangents, feedback, factors)
 
 
-def spread_kernel(replica_count, b3_ref, f3_ref, merged_ref, update_ref, rest_ref):
-    product = lax.dot_general(
-        b3_ref[0], f3_ref[0], (((0,), (0,)), ((), ())),
-        preferred_element_type=jnp.float32)
-    update = product / replica_count
-    update_ref[...] = update
-    rest_ref[0] = merged_ref[...] - update
-
-
-def spread(b3, f3, merged, replica_count):
+def spread_kernel(replica_count, b3_ref, fresh_ref, merged_ref, update_ref, rest_ref, next_ref):
+    next_ref[...] = fresh_ref[...]
+    width = fresh_ref.shape[3]
+    for m in range(fresh_ref.shape[1]):
+        hi, lo = halves(fresh_ref[0, m])
+        product = lax.dot_general(
+            b3_ref[m], jnp.concatenate([hi, lo, hi], axis=0), (((0,), (0,)), ((), ())),
+            preferred_element_type=jnp.float32)
+        update = product / replica_count
+        view = slice(m * width, (m + 1) * width)
+        update_ref[:, view] = update
+        rest_ref[0, :, view] = merged_ref[:, view] - update
+
+
+def spread(b3, fresh, merged, replica_count):
     rows, width = merged.shape
-    per = f3.shape[2] // COLS
-    cols = pl.BlockSpec((rows, COLS), lambda c: (0, c))
+    strip = 128 if rows % 128 == 0 else rows
+    strips = pl.BlockSpec((strip, width), lambda i: (i, 0))
+    whole = pl.BlockSpec(fresh.shape, lambda i: (0, 0, 0, 0))
     return pl.pallas_call(
         functools.partial(spread_kernel, replica_count),
-        grid=(width // COLS,),
+        grid=(rows // strip,),
         out_shape=[
             jax.ShapeDtypeStruct((rows, width), jnp.float32),
             jax.ShapeDtypeStruct((1, rows, width), jnp.float32),
+            jax.ShapeDtypeStruct(fresh.shape, jnp.float32),
         ],
         in_specs=[
-            pl.BlockSpec((1,) + b3.shape[1:], lambda c: (c // per, 0, 0)),
-            pl.BlockSpec((1, f3.shape[1], COLS), lambda c: (c // per, 0, c % per)),
-            cols,
+            pl.BlockSpec(b3.shape[:2] + (strip,), lambda i: (0, 0, i)),
+            whole,
+            strips,
         ],
-        out_specs=[cols, pl.BlockSpec((1, rows, COLS), lambda c: (0, 0, c))],
-        compiler_params=pltpu.CompilerParams(vmem_limit_bytes=32 * 2**20),
-    )(b3, f3, merged)
+        out_specs=[strips, pl.BlockSpec((1, strip, width), lambda i: (0, i, 0)), whole],
+        compiler_params=pltpu.CompilerParams(vmem_limit_bytes=58 * 2**20),
+    )(b3, fresh, merged)
 
 
 def body(features, cotangents, feedback, factors):
     grad_scale = 0.25 / math.sqrt(features.shape[0] * lax.axis_size("shard"))
-    merged, next_factors, b3, f3 = compress(
+    merged, fresh, b3 = compress(
         features, cotangents, feedback, factors, grad_scale)
-    update, new_feedback = spread(b3, f3, merged, lax.axis_size("replica"))
+    update, new_feedback, next_factors = spread(
+        b3, fresh, merged, lax.axis_size("replica"))
     return (update, new_feedback, next_factors)
 
 

time: 218 us -> 219 us (level)
  the two profiles are of different devices: /device:TPU:17 before, /device:TPU:0 now
where the time goes in v3:
time: 219 us
  Pallas kernels  218 us (100%)
    pallas_call x1, Pallas kernels, compress(): pl.pallas_call(functools.partial(merge_kernel, lines, scale, by_slice), o...  210 us
    pallas_call x1, Pallas kernels, spread(): pl.pallas_call(functools.partial(spread_kernel, replica_count), grid=(row...  8 us

profile of v3, /device:TPU:0, one launch (start us, length us, event | category | flops | bytes accessed | tf_op | source)
XLA Modules:
  0.0 218.9 jit_solution(16027237905995903415)
XLA Ops:
  0.6 210.2 %shard_map.67 = (f32[640,2048]{1,0:T(8,128)}, f32[1,2,32,1024]{3,2,1,0:T(8,128)}, bf16[2,96,640]{2,1,0:T(8,128)(2,1)}) custom-call(bf16[512,5120]{1,0:T(8,128)(2,1)} %x_ref.1, bf16[512,2048]{1,0:T(8,128)(2,1)} %g_ref.1, f32[1,640,2048]{2,1,0:T(8,128)} %fb_ref.1, f32[1,2,32,1024]{3,2,1,0:T(8,128)} %f_ref.1), custom_call_target="tpu_custom_call" | custom-call | flops 10737418240 | bytes 20971520 | tf_op jit(solution)/shard_map/pallas_call | solution.py:316
  210.9 8.0 %shard_map.68 = (f32[640,2048]{1,0:T(8,128)}, f32[1,640,2048]{2,1,0:T(8,128)}, f32[1,2,32,1024]{3,2,1,0:T(8,128)}) custom-call(bf16[2,96,640]{2,1,0:T(8,128)(2,1)} %get-tuple-element.6.b3_ref, f32[1,2,32,1024]{3,2,1,0:T(8,128)} %get-tuple-element.7.fresh_ref, f32[640,2048]{1,0:T(8,128)} %get-tuple-element.8.merged_ref), custom_call_target="tpu_custom_call" | custom-call | tf_op jit(solution)/shard_map/pallas_call | solution.py:370

commit v4 on v3

--- a/solution.py
+++ b/solution.py
@@ -183,27 +183,6 @@
 
         make(i).start()
 
-    @pl.loop(edge, last * chunks + last)
-    def _(t):
-        @pl.when(t - edge < chunks)
-        def _():
-            g_local(t - edge).wait()
-            g_remote(t - edge).wait()
-
-        i = t - z
-
-        @pl.when(jnp.logical_and(i >= 0, i < (last - z) * chunks))
-        def _():
-            relay(up, up_hop, up_send, i, last - i // chunks, i % chunks, z > 0)
-
-        j = t - (last - z)
-
-        @pl.when(jnp.logical_and(j >= 0, j < z * chunks))
-        def _():
-            relay(down, down_hop, down_send, j, j // chunks, j % chunks, z < last)
-
-    wait_x(z)
-    fb_copy.wait()
     left[...] = jnp.zeros_like(left)
 
     def out_copy(c):
@@ -211,8 +190,12 @@
         return pltpu.make_async_copy(
             acc.at[:, view], out_ref.at[:, view], out_sem.at[c])
 
-    @pl.loop(0, chunks)
-    def _(c):
+    def settle(c):
+        @pl.when(c == 0)
+        def _():
+            wait_x(z)
+            fb_copy.wait()
+
         view = pl.ds(pl.multiple_of(c * COLS, COLS), COLS)
         acc[:, view] += term(z, c)
 
@@ -237,6 +220,36 @@
             [jnp.where(member == m, part, 0.0) for m in range(members)], axis=0)
         f_hi, f_lo = halves(wide)
         left[...] += dot_t(hi, f_hi) + dot_t(hi, f_lo) + dot_t(lo, f_hi)
+
+    settle_at = jnp.where(
+        edge > 0,
+        jnp.maximum((last - z) * chunks + z, z * chunks + last - z),
+        (last - 1) * chunks)
+
+    @pl.loop(edge, last * chunks + last)
+    def _(t):
+        @pl.when(t - edge < chunks)
+        def _():
+            g_local(t - edge).wait()
+            g_remote(t - edge).wait()
+
+        i = t - z
+
+        @pl.when(jnp.logical_and(i >= 0, i < (last - z) * chunks))
+        def _():
+            relay(up, up_hop, up_send, i, last - i // chunks, i % chunks, z > 0)
+
+        j = t - (last - z)
+
+        @pl.when(jnp.logical_and(j >= 0, j < z * chunks))
+        def _():
+            relay(down, down_hop, down_send, j, j // chunks, j % chunks, z < last)
+
+        own = t - settle_at
+
+        @pl.when(jnp.logical_and(own >= 0, own < chunks))
+        def _():
+            settle(own)
 
     left_copy = pltpu.make_async_remote_copy(
         src_ref=left, dst_ref=left_in, send_sem=left_send, recv_sem=left_recv,
@@ -349,38 +362,41 @@
 
 
 def spread_kernel(replica_count, b3_ref, fresh_ref, merged_ref, update_ref, rest_ref, next_ref):
-    next_ref[...] = fresh_ref[...]
-    width = fresh_ref.shape[3]
-    for m in range(fresh_ref.shape[1]):
-        hi, lo = halves(fresh_ref[0, m])
-        product = lax.dot_general(
-            b3_ref[m], jnp.concatenate([hi, lo, hi], axis=0), (((0,), (0,)), ((), ())),
-            preferred_element_type=jnp.float32)
-        update = product / replica_count
-        view = slice(m * width, (m + 1) * width)
-        update_ref[:, view] = update
-        rest_ref[0, :, view] = merged_ref[:, view] - update
+    value = fresh_ref[...]
+    next_ref[...] = value
+    hi, lo = halves(value[0, 0])
+    product = lax.dot_general(
+        b3_ref[0], jnp.concatenate([hi, lo, hi], axis=0), (((0,), (0,)), ((), ())),
+        preferred_element_type=jnp.float32)
+    update = product / replica_count
+    update_ref[...] = update
+    rest_ref[0] = merged_ref[...] - update
 
 
 def spread(b3, fresh, merged, replica_count):
     rows, width = merged.shape
+    members, rank, kv_width = fresh.shape[1:]
     strip = 128 if rows % 128 == 0 else rows
-    strips = pl.BlockSpec((strip, width), lambda i: (i, 0))
-    whole = pl.BlockSpec(fresh.shape, lambda i: (0, 0, 0, 0))
+    strips = pl.BlockSpec((strip, kv_width), lambda m, i: (i, m))
+    member = pl.BlockSpec((1, 1, rank, kv_width), lambda m, i: (0, m, 0, 0))
     return pl.pallas_call(
         functools.partial(spread_kernel, replica_count),
-        grid=(rows // strip,),
+        grid=(members, rows // strip),
         out_shape=[
             jax.ShapeDtypeStruct((rows, width), jnp.float32),
             jax.ShapeDtypeStruct((1, rows, width), jnp.float32),
             jax.ShapeDtypeStruct(fresh.shape, jnp.float32),
         ],
         in_specs=[
-            pl.BlockSpec(b3.shape[:2] + (strip,), lambda i: (0, 0, i)),
-            whole,
+            pl.BlockSpec((1, b3.shape[1], strip), lambda m, i: (m, 0, i)),
+            member,
             strips,
         ],
-        out_specs=[strips, pl.BlockSpec((1, strip, width), lambda i: (0, i, 0)), whole],
+        out_specs=[
+            strips,
+            pl.BlockSpec((1, strip, kv_width), lambda m, i: (0, i, m)),
+            member,
+        ],
         compiler_params=pltpu.CompilerParams(vmem_limit_bytes=58 * 2**20),
     )(b3, fresh, merged)
 

time: 219 us -> 215 us (0.982)
  the two profiles are of different devices: /device:TPU:0 before, /device:TPU:17 now
where the time goes in v4:
time: 215 us
  Pallas kernels  214 us (100%)
    pallas_call x1, Pallas kernels, compress(): pl.pallas_call(functools.partial(merge_kernel, lines, scale, by_slice), o...  204 us
    pallas_call x1, Pallas kernels, spread(): pl.pallas_call(functools.partial(spread_kernel, replica_count), grid=(mem...  10.1 us

profile of v4, /device:TPU:17, one launch (start us, length us, event | category | flops | bytes accessed | tf_op | source)
XLA Modules:
  0.0 214.8 jit_solution(7641744658125862159)
XLA Ops:
  0.6 204.1 %shard_map.67 = (f32[640,2048]{1,0:T(8,128)}, f32[1,2,32,1024]{3,2,1,0:T(8,128)}, bf16[2,96,640]{2,1,0:T(8,128)(2,1)}) custom-call(bf16[512,5120]{1,0:T(8,128)(2,1)} %x_ref.1, bf16[512,2048]{1,0:T(8,128)(2,1)} %g_ref.1, f32[1,640,2048]{2,1,0:T(8,128)} %fb_ref.1, f32[1,2,32,1024]{3,2,1,0:T(8,128)} %f_ref.1), custom_call_target="tpu_custom_call" | custom-call | flops 10737418240 | bytes 20971520 | tf_op jit(solution)/shard_map/pallas_call | solution.py:329
  204.7 10.1 %shard_map.68 = (f32[640,2048]{1,0:T(8,128)}, f32[1,640,2048]{2,1,0:T(8,128)}, f32[1,2,32,1024]{3,2,1,0:T(8,128)}) custom-call(bf16[2,96,640]{2,1,0:T(8,128)(2,1)} %get-tuple-element.6.b3_ref, f32[1,2,32,1024]{3,2,1,0:T(8,128)} %get-tuple-element.7.fresh_ref, f32[640,2048]{1,0:T(8,128)} %get-tuple-element.8.merged_ref), custom_call_target="tpu_custom_call" | custom-call | tf_op jit(solution)/shard_map/pallas_call | solution.py:382

commit v5 on v4

--- a/solution.py
+++ b/solution.py
@@ -375,28 +375,24 @@
 
 def spread(b3, fresh, merged, replica_count):
     rows, width = merged.shape
-    members, rank, kv_width = fresh.shape[1:]
-    strip = 128 if rows % 128 == 0 else rows
-    strips = pl.BlockSpec((strip, kv_width), lambda m, i: (i, m))
-    member = pl.BlockSpec((1, 1, rank, kv_width), lambda m, i: (0, m, 0, 0))
+    rank, kv_width = fresh.shape[2:]
+    per = kv_width // WIDE
+    cols = pl.BlockSpec((rows, WIDE), lambda c: (0, c))
+    right = pl.BlockSpec((1, 1, rank, WIDE), lambda c: (0, c // per, 0, c % per))
     return pl.pallas_call(
         functools.partial(spread_kernel, replica_count),
-        grid=(members, rows // strip),
+        grid=(width // WIDE,),
         out_shape=[
             jax.ShapeDtypeStruct((rows, width), jnp.float32),
             jax.ShapeDtypeStruct((1, rows, width), jnp.float32),
             jax.ShapeDtypeStruct(fresh.shape, jnp.float32),
         ],
         in_specs=[
-            pl.BlockSpec((1, b3.shape[1], strip), lambda m, i: (m, 0, i)),
-            member,
-            strips,
+            pl.BlockSpec((1,) + b3.shape[1:], lambda c: (c // per, 0, 0)),
+            right,
+            cols,
         ],
-        out_specs=[
-            strips,
-            pl.BlockSpec((1, strip, kv_width), lambda m, i: (0, i, m)),
-            member,
-        ],
+        out_specs=[cols, pl.BlockSpec((1, rows, WIDE), lambda c: (0, 0, c)), right],
         compiler_params=pltpu.CompilerParams(vmem_limit_bytes=58 * 2**20),
     )(b3, fresh, merged)
 

time: 215 us -> 214 us (level)
  no operation moved by 1% of the time
where the time goes in v5:
time: 214 us
  Pallas kernels  213 us (100%)
    pallas_call x1, Pallas kernels, compress(): pl.pallas_call(functools.partial(merge_kernel, lines, scale, by_slice), o...  204 us
    pallas_call x1, Pallas kernels, spread(): pl.pallas_call(functools.partial(spread_kernel, replica_count), grid=(wid...  9.26 us

profile of v5, /device:TPU:17, one launch (start us, length us, event | category | flops | bytes accessed | tf_op | source)
XLA Modules:
  0.0 214.0 jit_solution(13185186214025055874)
XLA Ops:
  0.6 204.1 %shard_map.67 = (f32[640,2048]{1,0:T(8,128)}, f32[1,2,32,1024]{3,2,1,0:T(8,128)}, bf16[2,96,640]{2,1,0:T(8,128)(2,1)}) custom-call(bf16[512,5120]{1,0:T(8,128)(2,1)} %x_ref.1, bf16[512,2048]{1,0:T(8,128)(2,1)} %g_ref.1, f32[1,640,2048]{2,1,0:T(8,128)} %fb_ref.1, f32[1,2,32,1024]{3,2,1,0:T(8,128)} %f_ref.1), custom_call_target="tpu_custom_call" | custom-call | flops 10737418240 | bytes 20971520 | tf_op jit(solution)/shard_map/pallas_call | solution.py:329
  204.7 9.3 %shard_map.68 = (f32[640,2048]{1,0:T(8,128)}, f32[1,640,2048]{2,1,0:T(8,128)}, f32[1,2,32,1024]{3,2,1,0:T(8,128)}) custom-call(bf16[2,96,640]{2,1,0:T(8,128)(2,1)} %get-tuple-element.6.b3_ref, f32[1,2,32,1024]{3,2,1,0:T(8,128)} %get-tuple-element.7.fresh_ref, f32[640,2048]{1,0:T(8,128)} %get-tuple-element.8.merged_ref), custom_call_target="tpu_custom_call" | custom-call | tf_op jit(solution)/shard_map/pallas_call | solution.py:382
